TPU v7x, 32 devices: a whole 2x2x4 slice. The times are simulated.
32 devices in a mesh: member: 2 (over x), lon: 16 (over z, y, core).
Axes of the slice: x: 2, y: 2, z: 4, core: 2. Of those that a mesh axis runs over, the one named last changes fastest.
Arguments:
- tracer_field: float32 [16, 2, 192, 768], P('member', None, 'lon'), parts along dimension 0, may hold values from -6 to 6
- courant_lon: float32 [4, 192, 768], P('member', 'lon'), parts along dimension 0, may hold values from -0.4 to 0.4
- courant_lat: float32 [4, 192, 768], P('member', 'lon'), parts along dimension 0, may hold values from -0.4 to 0.4
- diffusivity: float32 [2, 192, 768], P('member', 'lon'), parts along dimension 0, may hold values from 0.1 to 4
- polar_mask: int32 [768], replicated, may hold values from 0 to 1, as said below
- cutoff: int32 [768], replicated, may hold values from 4 to 95, as said below
Outputs:
- updated_field: float32 [16, 2, 192, 768], P('member', None, 'lon'), parts along dimension 0
There are 2 independent parts, one for each index of `member`. A program takes and returns all parts, laid end to end along the dimension named above; an argument that names none is the same for every part. Nothing has to cross between parts.
Inputs may be any that keep to these rules, and one draw needn't show every extreme that they name: `polar_mask`: 1 on the first 128 rows and on a last run of 64 to 128 rows, 0 elsewhere. `cutoff`: only rows with mask 1 use it.
All inputs are finite; a program needn't handle non-finite values.
Results may differ from a plain program's by a relative error of at most 0.00005.
Values sent between devices are 32-bit elements; how exact they have to be, the bound alone decides.
A program may use at most 128 MiB of HBM per device.

v0:
```python
import math
import jax
import jax.numpy as jnp
from jax import lax
from jax.sharding import PartitionSpec as P


def padded(x, sides, width):
    for axis, dim in sides:
        size, length = (lax.axis_size(axis), x.shape[dim])
        up = [(i, (i + 1) % size) for i in range(size)]
        down = [(j, i) for i, j in up]
        last = lax.slice_in_dim(x, length - width, length, axis=dim)
        leading = lax.slice_in_dim(x, 0, width, axis=dim)
        before = lax.ppermute(last, axis, up)
        after = lax.ppermute(leading, axis, down)
        x = jnp.concatenate([before, x, after], axis=dim)
    return x


def vertical_solve(diffusivity, field):
    levels = field.shape[1]
    zeros_plane = jnp.zeros_like(diffusivity[0])
    upper_list = []
    rhs_list = []
    prev_upper = None
    prev_rhs = None
    for lev_index in range(levels):
        below = diffusivity[lev_index - 1] if lev_index > 0 else zeros_plane
        above = diffusivity[lev_index] if lev_index < levels - 1 else zeros_plane
        diagonal = 1.0 + below + above
        source = field[:, lev_index]
        if lev_index == 0:
            denom = diagonal
            new_rhs = source / denom
        else:
            denom = diagonal + below * prev_upper
            new_rhs = (source + below * prev_rhs) / denom
        new_upper = -above / denom
        upper_list.append(new_upper)
        rhs_list.append(new_rhs)
        prev_upper = new_upper
        prev_rhs = new_rhs
    result = [None] * levels
    current = rhs_list[levels - 1]
    result[levels - 1] = current
    lev_index = 0
    current = rhs_list[lev_index] - upper_list[lev_index] * current
    result[lev_index] = current
    return jnp.stack(result, axis=1)


def fourier_tables(length):
    half_len = length // 2
    column = jnp.arange(length, dtype=jnp.int32)[:, None]
    wavenum = jnp.arange(1, half_len + 1, dtype=jnp.int32)[None, :]
    phase = column * wavenum % length
    angle = 2.0 * math.pi / length * phase.astype(jnp.float32)
    return (jnp.cos(angle), jnp.sin(angle))


def high_part(block, row_cut, cosine, sine):
    length = block.shape[1]
    half_len = length // 2
    highest = lax.Precision.HIGHEST
    real_part = jnp.einsum("bir,im->brm", block, cosine, precision=highest)
    imag_part = jnp.einsum("bir,im->brm", block, sine, precision=highest)
    wavenum = jnp.arange(1, half_len + 1, dtype=jnp.int32)
    weights = jnp.where(wavenum == half_len, 1.0 / length, 2.0 / length).astype(jnp.float32)
    keeper = jnp.where(wavenum[None, :] > row_cut[:, None], weights[None, :], 0.0)
    return jnp.einsum(
        "brm,im->bir", real_part * keeper[None], cosine, precision=highest
    ) + jnp.einsum("brm,im->bir", imag_part * keeper[None], sine, precision=highest)


def local(tracer_field, courant_lon, courant_lat, diffusivity, polar_mask, cutoff):
    tracers, levels, lon_local, lat_rows = tracer_field.shape
    zero_row = jnp.zeros_like(tracer_field[..., :1])
    north_next = jnp.concatenate([tracer_field[..., 1:], zero_row], axis=3)
    north = (
        jnp.maximum(courant_lat, 0.0)[None] * tracer_field
        + jnp.minimum(courant_lat, 0.0)[None] * north_next
    )
    south = jnp.concatenate([zero_row, north[..., :-1]], axis=3)
    stacked = jnp.concatenate([tracer_field, courant_lon[None]], axis=0)
    extended = padded(stacked, (("lon", 2),), 1)
    tracer_ext = extended[:tracers]
    speed_ext = extended[tracers][None, :, :-1]
    east_all = (
        jnp.maximum(speed_ext, 0.0) * tracer_ext[:, :, :-1]
        + jnp.minimum(speed_ext, 0.0) * tracer_ext[:, :, 1:]
    )
    east = east_all[:, :, 1:]
    west = east_all[:, :, :-1]
    advected = tracer_field - (east - west) - (north - south)
    batched = advected.reshape(tracers * levels, lon_local, lat_rows)
    length = lon_local * lax.axis_size("lon")
    cosine, sine = fourier_tables(length)
    mask_float = polar_mask.astype(jnp.float32)
    row_count = lat_rows // lax.axis_size("lon")
    first_row = lax.axis_index("lon") * row_count
    my_cut = lax.dynamic_slice_in_dim(cutoff, first_row, row_count)
    my_mask = lax.dynamic_slice_in_dim(mask_float, first_row, row_count)
    removed = (
        high_part(
            lax.all_to_all(batched, "lon", split_axis=2, concat_axis=1, tiled=True),
            my_cut,
            cosine,
            sine,
        )
        * my_mask[None, None, :]
    )
    correction = lax.all_to_all(removed, "lon", split_axis=1, concat_axis=2, tiled=True)
    filtered = (batched - correction).reshape(tracers, levels, lon_local, lat_rows)
    return vertical_solve(diffusivity, filtered)


def solution(mesh):
    placed = (
        P("member", None, "lon", None),
        P("member", "lon", None),
        P("member", "lon", None),
        P("member", "lon", None),
        P(),
        P(),
    )
    return jax.shard_map(
        local, mesh=mesh, in_specs=placed, out_specs=P("member", None, "lon", None), check_vma=False
    )
```

profile of v0, /device:TPU:0, one launch (start us, length us, event | category | flops | bytes accessed | tf_op | source)
XLA Modules:
  0.0 89.5 jit_solution(6929786615368778992)
XLA Ops:
  0.0 1.0 %pad_maximum_fusion.9 = (f32[9,2,1,768]{3,1,0,2:T(2,128)S(1)}, f32[9,2,1,768]{3,1,0,2:T(2,128)S(1)}) fusion(f32[1,2,12,768]{3,1,0,2:T(2,128)} %bitcast.52, f32[8,2,12,768]{3,1,2,0:T(2,128)} %param.6), kind=kLoop, calls=%fused_computation.42 | loop fusion | flops 27648 | bytes 774144 | tf_op jit(solution)/shard_map/slice | solution.py:13
  1.0 0.5 collective-permute-start
  1.5 5.1 %collective-permute-start.1 = (f32[9,2,1,768]{3,1,0,2:T(2,128)S(1)}, f32[9,2,1,768]{3,1,0,2:T(2,128)S(1)}, u32[]{:S(2)}, u32[]{:S(2)}) collective-permute-start(f32[9,2,1,768]{3,1,0,2:T(2,128)S(1)} %get-tuple-element.10), channel_id=1, source_target_pairs={{1,0},{2,1},{3,2},{4,3},{5,4},{6,5},{7,6},{8,7},{9,8},{10,9},{11,1... | collective-permute-start | bytes 165896 | tf_op jit(solution)/shard_map/ppermute | solution.py:16
  6.5 1.7 %slice.56 = f32[8,2,12,767]{3,1,2,0:T(2,128)S(1)} slice(f32[8,2,12,768]{3,1,2,0:T(2,128)} %param.6), slice={[0:8], [0:2], [0:12], [1:768]} | slice | bytes 1178112 | tf_op jit(solution)/shard_map/slice | solution.py:79
  8.5 0.4 multiply_add_fusion
  9.8 0.8 fusion.6
  10.6 0.4 reshape.61
  11.0 5.0 %copy.19 = f32[16,12,768]{0,1,2:T(8,128)} copy(f32[16,12,768]{2,0,1:T(8,128)S(1)} %reshape.61) | data formatting | bytes 1179648 | tf_op jit(solution)/shard_map/reshape | solution.py:96
  16.0 5.5 %reshape.64 = f32[16,1,9216]{2,1,0:T(1,128)} reshape(f32[768,12,16]{2,1,0:T(8,128)} %bitcast.46) | data formatting | bytes 1179648
  21.4 5.0 %all-to-all-start = ((f32[16,1,9216]{2,1,0:T(1,128)}), f32[16,1,9216]{2,1,0:T(1,128)S(1)}, u32[]{:S(2)}, u32[]{:S(2)}) async-start(f32[16,1,9216]{2,1,0:T(1,128)} %reshape.64), calls=%async_computation | async-start | bytes 1179648 | tf_op jit(solution)/shard_map/all_to_all | solution.py:106
  26.4 0.8 dynamic_slice.6
  27.4 14.6 %all-to-all-done = f32[16,1,9216]{2,1,0:T(1,128)S(1)} async-done(((f32[16,1,9216]{2,1,0:T(1,128)}), f32[16,1,9216]{2,1,0:T(1,128)S(1)}, u32[]{:S(2)}, u32[]{:S(2)}) %all-to-all-start) | async-done | bytes 589856 | tf_op jit(solution)/shard_map/all_to_all | solution.py:106
  42.0 0.5 broadcast.105
  42.5 1.9 %reduce = f32[16,9216]{1,0:T(8,128)S(1)} reduce(f32[16,1,9216]{2,1,0:T(1,128)S(1)} %all-to-all-done, f32[]{:T(128)} %broadcast.105), dimensions={1}, to_apply=%all_to_all.26.reduce_sub_computation | reduce | bytes 1179652 | tf_op jit(solution)/shard_map/all_to_all | solution.py:106
  44.4 4.4 %reshape.65 = f32[768,12,16]{2,1,0:T(8,128)} reshape(f32[16,9216]{1,0:T(8,128)S(1)} %reduce) | data formatting | bytes 1179648
  48.8 4.7 %copy.21 = f32[16,16,12,48]{3,0,2,1:T(8,128)S(1)} copy(f32[16,16,12,48]{0,2,3,1:T(8,128)} %bitcast.47) | data formatting | bytes 1179648 | tf_op jit(solution)/shard_map/all_to_all | solution.py:106
  53.5 0.8 copy.22
  54.3 1.2 %convolution_multiply_fusion.1 = f32[16,48,96]{2,1,0:T(8,128)S(1)} fusion(f32[16,192,48]{1,2,0:T(8,128)S(1)} %copy.22, f32[48,96]{1,0:T(8,128)S(1)} %compare_select_fusion, s32[96]{0:T(128)S(1)} %iota_add_fusion), kind=kOutput, calls=%fused_computation.4 | convolution fusion | flops 170108928 | bytes 903552 | tf_op jit(solution)/shard_map/bir,im->brm/dot_general | solution.py:66
  55.4 1.2 %convolution_multiply_fusion = f32[16,48,96]{2,1,0:T(8,128)S(1)} fusion(f32[16,192,48]{1,2,0:T(8,128)S(1)} %copy.22, f32[48,96]{1,0:T(8,128)S(1)} %compare_select_fusion, s32[96]{0:T(128)S(1)} %iota_add_fusion), kind=kOutput, calls=%fused_computation.3 | convolution fusion | flops 170108928 | bytes 903552 | tf_op jit(solution)/shard_map/bir,im->brm/dot_general | solution.py:67
  56.6 1.2 %fusion.12 = f32[192,16,48]{0,2,1:T(8,128)S(1)} fusion(f32[16,48,96]{2,1,0:T(8,128)S(1)} %convolution_multiply_fusion.1, s32[96]{0:T(128)S(1)} %iota_add_fusion), kind=kOutput, calls=%fused_computation.26 | convolution fusion | flops 170035200 | bytes 885120 | tf_op jit(solution)/shard_map/brm,im->bir/dot_general | solution.py:71
  57.8 1.2 %fusion.1 = f32[16,192,48]{1,2,0:T(8,128)S(1)} fusion(f32[192,16,48]{0,2,1:T(8,128)S(1)} %fusion.12, f32[16,48,96]{2,1,0:T(8,128)S(1)} %convolution_multiply_fusion, f32[48]{0:T(128)S(1)} %dynamic_slice.7, s32[96]{0:T(128)S(1)} %iota_add_fusion), kind=kOutput, calls=%fused_computation.2 | convolution fusion | flops 170330112 | bytes 1475136 | tf_op jit(solution)/shard_map/brm,im->bir/dot_general | solution.py:73
  58.9 0.8 copy.24
  59.8 2.4 %reshape.66 = f32[16,1,9216]{2,1,0:T(1,128)} reshape(f32[192,16,48]{2,1,0:T(8,128)S(1)} %bitcast.48) | data formatting | bytes 1179648
  62.2 4.4 %all-to-all-start.1 = ((f32[16,1,9216]{2,1,0:T(1,128)}), f32[16,1,9216]{2,1,0:T(1,128)S(1)}, u32[]{:S(2)}, u32[]{:S(2)}) async-start(f32[16,1,9216]{2,1,0:T(1,128)} %reshape.66), calls=%async_computation.1 | async-start | bytes 1179648 | tf_op jit(solution)/shard_map/all_to_all | solution.py:113
  66.7 15.4 %all-to-all-done.1 = f32[16,1,9216]{2,1,0:T(1,128)S(1)} async-done(((f32[16,1,9216]{2,1,0:T(1,128)}), f32[16,1,9216]{2,1,0:T(1,128)S(1)}, u32[]{:S(2)}, u32[]{:S(2)}) %all-to-all-start.1) | async-done | bytes 589856 | tf_op jit(solution)/shard_map/all_to_all | solution.py:113
  82.2 2.0 %reduce.1 = f32[16,9216]{1,0:T(8,128)S(1)} reduce(f32[16,1,9216]{2,1,0:T(1,128)S(1)} %all-to-all-done.1, f32[]{:T(128)} %broadcast.105), dimensions={1}, to_apply=%all_to_all.30.reduce_sub_computation | reduce | bytes 1179652 | tf_op jit(solution)/shard_map/all_to_all | solution.py:113
  84.1 0.7 reshape.67
  84.8 0.9 %copy.25 = f32[16,12,16,48]{3,2,0,1:T(8,128)S(1)} copy(f32[16,12,16,48]{3,0,1,2:T(8,128)S(1)} %bitcast.49) | data formatting | bytes 1179648 | tf_op jit(solution)/shard_map/all_to_all | solution.py:113
  85.7 1.3 %all_to_all.33 = f32[8,2,12,768]{3,1,0,2:T(2,128)S(1)} reshape(f32[16,12,16,48]{3,2,0,1:T(8,128)S(1)} %copy.25) | data formatting | bytes 1179648 | tf_op jit(solution)/shard_map/all_to_all | solution.py:113
  87.4 0.7 multiply_subtract_fusion
  88.0 0.5 pad_maximum_fusion.4
  88.6 0.9 copy.26
  (30 shorter events, 1.6 us)
Async XLA Ops:
  0.0 8.3 %copy-start.5 = (f32[2,12,768]{2,0,1:T(2,128)S(1)}, f32[2,12,768]{2,0,1:T(2,128)}, u32[]{:S(2)}) copy-start(f32[2,12,768]{2,0,1:T(2,128)} %param.8) | copy-start | bytes 221188
  0.0 8.4 %copy-start = (f32[8,2,12,768]{3,1,2,0:T(2,128)S(1)}, f32[8,2,12,768]{3,1,2,0:T(2,128)}, u32[]{:S(2)}) copy-start(f32[8,2,12,768]{3,1,2,0:T(2,128)} %param.6) | copy-start | bytes 1769476
  1.0 7.9 %collective-permute-start = (f32[9,2,1,768]{3,1,0,2:T(2,128)S(1)}, f32[9,2,1,768]{3,1,0,2:T(2,128)S(1)}, u32[]{:S(2)}, u32[]{:S(2)}) collective-permute-start(f32[9,2,1,768]{3,1,0,2:T(2,128)S(1)} %get-tuple-element.9), channel_id=1, source_target_pairs={{0,1},{1,2},{2,3},{3,4},{4,5},{5,6},{6,7},{7,8},{8,9},{9,10},{10,1... | collective-permute-start | bytes 165896 | tf_op jit(solution)/shard_map/ppermute | solution.py:15
  1.5 7.4 %collective-permute-start.1 = (f32[9,2,1,768]{3,1,0,2:T(2,128)S(1)}, f32[9,2,1,768]{3,1,0,2:T(2,128)S(1)}, u32[]{:S(2)}, u32[]{:S(2)}) collective-permute-start(f32[9,2,1,768]{3,1,0,2:T(2,128)S(1)} %get-tuple-element.10), channel_id=1, source_target_pairs={{1,0},{2,1},{3,2},{4,3},{5,4},{6,5},{7,6},{8,7},{9,8},{10,9},{11,1... | collective-permute-start | bytes 165896 | tf_op jit(solution)/shard_map/ppermute | solution.py:16
  8.4 0.9 copy-start.3
  10.5 5.4 %copy-start.1 = (f32[8,2,12,768]{3,1,0,2:T(2,128)}, f32[8,2,12,768]{3,1,0,2:T(2,128)S(1)}, u32[]{:S(2)}) copy-start(f32[8,2,12,768]{3,1,0,2:T(2,128)S(1)} %fusion.6) | copy-start | bytes 1769476
  16.0 10.5 %copy-start.6 = (s32[768]{0:T(1024)S(1)}, s32[768]{0:T(1024)}, u32[]{:S(2)}) copy-start(s32[768]{0:T(1024)} %param.10) | copy-start | bytes 9220
  21.4 20.5 %all-to-all-start = ((f32[16,1,9216]{2,1,0:T(1,128)}), f32[16,1,9216]{2,1,0:T(1,128)S(1)}, u32[]{:S(2)}, u32[]{:S(2)}) async-start(f32[16,1,9216]{2,1,0:T(1,128)} %reshape.64), calls=%async_computation | async-start | bytes 1179648 | tf_op jit(solution)/shard_map/all_to_all | solution.py:106
  59.8 6.8 %copy-start.4 = (f32[1,12,768]{2,0,1:T(1,128)S(1)}, f32[1,12,768]{2,0,1:T(1,128)}, u32[]{:S(2)}) copy-start(f32[1,12,768]{2,0,1:T(1,128)} %param.9) | copy-start | bytes 110596
  62.2 20.0 %all-to-all-start.1 = ((f32[16,1,9216]{2,1,0:T(1,128)}), f32[16,1,9216]{2,1,0:T(1,128)S(1)}, u32[]{:S(2)}, u32[]{:S(2)}) async-start(f32[16,1,9216]{2,1,0:T(1,128)} %reshape.66), calls=%async_computation.1 | async-start | bytes 1179648 | tf_op jit(solution)/shard_map/all_to_all | solution.py:113
  85.7 1.3 %copy-start.2 = (f32[8,2,12,768]{3,1,0,2:T(2,128)S(1)}, f32[8,2,12,768]{3,1,0,2:T(2,128)}, u32[]{:S(2)}) copy-start(f32[8,2,12,768]{3,1,0,2:T(2,128)} %copy-done.1) | copy-start | bytes 1769476
where the time goes:
time: 90 us; the launch traced here: 89.5 us
  local copies, waits for them, and re-layouts  31.3 us (35%)
  waiting for transfers between devices  30 us (33%)
  starting transfers between devices  15 us (17%)
  other arithmetic  8.27 us (9%)
  matrix products  4.66 us (5%)
    all_to_all x1, waiting for transfers between devices, local(): lax.all_to_all(removed, 'lon', split_axis=1, concat_axis=2, tiled=True)  15.4 us
    all_to_all x1, waiting for transfers between devices, local(): lax.all_to_all(batched, 'lon', split_axis=2, concat_axis=1, tiled=True)  14.6 us
    unnamed x21, local copies, waits for them, and re-layouts  13.4 us
    all_to_all x3, local copies, waits for them, and re-layouts, local(): lax.all_to_all(batched, 'lon', split_axis=2, concat_axis=1, tiled=True)  5.92 us
    reshape x2, local copies, waits for them, and re-layouts, local(): batched = advected.reshape(tracers * levels, lon_local, lat_rows)  5.38 us
    ppermute x1, starting transfers between devices, padded(): after = lax.ppermute(leading, axis, down)  5.06 us
    all_to_all x1, starting transfers between devices, local(): lax.all_to_all(batched, 'lon', split_axis=2, concat_axis=1, tiled=True)  4.97 us
    all_to_all x1, starting transfers between devices, local(): lax.all_to_all(removed, 'lon', split_axis=1, concat_axis=2, tiled=True)  4.43 us
  transfers between devices with their start and end apart: 4, of which 2 were waited for; matrix products, arithmetic and copies ran while one was open for 4% of the time, Pallas kernels for 0%

commit v1 on v0

--- a/solution.py
+++ b/solution.py
@@ -3,6 +3,12 @@
 import jax.numpy as jnp
 from jax import lax
 from jax.sharding import PartitionSpec as P
+
+
+def trade_parts(shard, axis, split, join):
+    pieces = jnp.split(shard, lax.axis_size(axis), axis=split)
+    received = lax.all_to_all(jnp.stack(pieces), axis, 0, 0)
+    return jnp.concatenate(received, axis=join)
 
 
 def padded(x, sides, width):
@@ -102,13 +108,7 @@
     my_cut = lax.dynamic_slice_in_dim(cutoff, first_row, row_count)
     my_mask = lax.dynamic_slice_in_dim(mask_float, first_row, row_count)
     removed = (
-        high_part(
-            lax.all_to_all(batched, "lon", split_axis=2, concat_axis=1, tiled=True),
-            my_cut,
-            cosine,
-            sine,
-        )
-        * my_mask[None, None, :]
+        high_part(trade_parts(batched, "lon", 2, 1), my_cut, cosine, sine) * my_mask[None, None, :]
     )
     correction = lax.all_to_all(removed, "lon", split_axis=1, concat_axis=2, tiled=True)
     filtered = (batched - correction).reshape(tracers, levels, lon_local, lat_rows)

time: 90 us -> 75 us (0.83)
  local copies, waits for them, and re-layouts: 31.3 us -> 16.1 us
    unnamed x21 -> x36, local copies, waits for them, and re-layouts: 13.4 us -> 7.7 us
    all_to_all x3 -> x1, local copies, waits for them, and re-layouts: 5.92 us -> 0.57 us  [trade_parts(): received = lax.all_to_all(jnp.stack(pieces), axis, 0, 0)]
    reshape x2 -> x1, local copies, waits for them, and re-layouts: 5.38 us -> 0.41 us  [local(): batched = advected.reshape(tracers * levels, lon_local, lat_rows)]
where the time goes in v1:
time: 75 us; the launch traced here: 74.5 us
  waiting for transfers between devices  30 us (40%)
  local copies, waits for them, and re-layouts  16.1 us (21%)
  starting transfers between devices  15 us (20%)
  other arithmetic  8.4 us (11%)
  matrix products  4.66 us (6%)
    all_to_all x1, waiting for transfers between devices, local(): lax.all_to_all(removed, 'lon', split_axis=1, concat_axis=2, tiled=True)  15.4 us
    all_to_all x1, waiting for transfers between devices, trade_parts(): received = lax.all_to_all(jnp.stack(pieces), axis, 0, 0)  14.6 us
    unnamed x36, local copies, waits for them, and re-layouts  7.7 us
    ppermute x1, starting transfers between devices, padded(): after = lax.ppermute(leading, axis, down)  5.06 us
    all_to_all x1, starting transfers between devices, trade_parts(): received = lax.all_to_all(jnp.stack(pieces), axis, 0, 0)  4.97 us
    all_to_all x1, starting transfers between devices, local(): lax.all_to_all(removed, 'lon', split_axis=1, concat_axis=2, tiled=True)  4.43 us
    all_to_all x2, local copies, waits for them, and re-layouts, local(): lax.all_to_all(removed, 'lon', split_axis=1, concat_axis=2, tiled=True)  2.25 us
    all_to_all x1, other arithmetic, local(): lax.all_to_all(removed, 'lon', split_axis=1, concat_axis=2, tiled=True)  2.01 us
  transfers between devices with their start and end apart: 4, of which 2 were waited for; matrix products, arithmetic and copies ran while one was open for 4% of the time, Pallas kernels for 0%

profile of v1, /device:TPU:0, one launch (start us, length us, event | category | flops | bytes accessed | tf_op | source)
XLA Modules:
  0.0 74.5 jit_solution(2181363217038815638)
XLA Ops:
  0.0 1.0 %pad_maximum_fusion.9 = (f32[9,2,1,768]{3,1,0,2:T(2,128)S(1)}, f32[9,2,1,768]{3,1,0,2:T(2,128)S(1)}) fusion(f32[1,2,12,768]{3,1,0,2:T(2,128)} %bitcast.113, f32[8,2,12,768]{3,1,2,0:T(2,128)} %param.6), kind=kLoop, calls=%fused_computation.74 | loop fusion | flops 27648 | bytes 774144 | tf_op jit(solution)/shard_map/slice | solution.py:19
  1.0 0.5 collective-permute-start
  1.5 5.1 %collective-permute-start.1 = (f32[9,2,1,768]{3,1,0,2:T(2,128)S(1)}, f32[9,2,1,768]{3,1,0,2:T(2,128)S(1)}, u32[]{:S(2)}, u32[]{:S(2)}) collective-permute-start(f32[9,2,1,768]{3,1,0,2:T(2,128)S(1)} %get-tuple-element.10), channel_id=1, source_target_pairs={{1,0},{2,1},{3,2},{4,3},{5,4},{6,5},{7,6},{8,7},{9,8},{10,9},{11,1... | collective-permute-start | bytes 165896 | tf_op jit(solution)/shard_map/ppermute | solution.py:22
  6.5 1.7 %slice.56 = f32[8,2,12,767]{3,1,2,0:T(2,128)S(1)} slice(f32[8,2,12,768]{3,1,2,0:T(2,128)} %param.6), slice={[0:8], [0:2], [0:12], [1:768]} | slice | bytes 1178112 | tf_op jit(solution)/shard_map/slice | solution.py:85
  8.5 0.4 multiply_add_fusion
  8.9 0.3 copy-done.3
  9.4 0.4 fusion.3
  9.8 0.8 %fusion.6 = f32[8,2,12,768]{3,1,0,2:T(2,128)S(1)} fusion(f32[8,2,13,768]{3,1,0,2:T(2,128)S(1)} %fusion.3, f32[8,2,12,768]{3,1,0,2:T(2,128)S(1)} %multiply_add_fusion, f32[8,2,12,767]{3,1,0,2:T(2,128)S(1)} %bitcast.111, f32[8,2,12,768]{3,1,2,0:T(2,128)S(1)} %copy-done), kind=kLoop, calls=%fused_computation.14 | loop fusion | flops 589824 | bytes 3538176 | tf_op jit(solution)/shard_map/sub | solution.py:101
  10.6 0.4 reshape.67
  12.3 2.4 %reshape.72 = f32[16,1,9216]{2,1,0:T(1,128)} reshape(f32[16,12,16,48]{3,2,1,0:T(8,128)S(1)} %bitcast.112) | data formatting | bytes 1179648
  14.7 5.0 %all-to-all-start = ((f32[16,1,9216]{2,1,0:T(1,128)}), f32[16,1,9216]{2,1,0:T(1,128)S(1)}, u32[]{:S(2)}, u32[]{:S(2)}) async-start(f32[16,1,9216]{2,1,0:T(1,128)} %reshape.72), calls=%async_computation | async-start | bytes 1179648 | tf_op jit(solution)/shard_map/all_to_all | solution.py:10
  19.7 0.8 %dynamic_slice.6 = s32[48]{0:T(128)S(1)} dynamic-slice(s32[768]{0:T(1024)} %param.11, s32[]{:T(128)S(6)} %select_n.34), dynamic_slice_sizes={48} | dynamic-slice | bytes 388 | tf_op jit(solution)/shard_map/dynamic_slice | solution.py:108
  20.6 14.6 %all-to-all-done = f32[16,1,9216]{2,1,0:T(1,128)S(1)} async-done(((f32[16,1,9216]{2,1,0:T(1,128)}), f32[16,1,9216]{2,1,0:T(1,128)S(1)}, u32[]{:S(2)}, u32[]{:S(2)}) %all-to-all-start) | async-done | bytes 589856 | tf_op jit(solution)/shard_map/all_to_all | solution.py:10
  35.2 0.6 broadcast.105
  35.8 2.0 %reduce = f32[16,9216]{1,0:T(8,128)S(1)} reduce(f32[16,1,9216]{2,1,0:T(1,128)S(1)} %all-to-all-done, f32[]{:T(128)} %broadcast.105), dimensions={1}, to_apply=%all_to_all.16.reduce_sub_computation | reduce | bytes 1179652 | tf_op jit(solution)/shard_map/all_to_all | solution.py:10
  37.8 0.7 reshape.73
  38.5 0.8 %copy.18 = f32[16,192,48]{1,2,0:T(8,128)S(1)} copy(f32[16,192,48]{2,0,1:T(8,128)S(1)} %bitcast.108) | data formatting | bytes 1179648 | tf_op jit(solution)/shard_map/reshape | solution.py:11
  39.3 1.2 %convolution_multiply_fusion.1 = f32[16,48,96]{2,1,0:T(8,128)S(1)} fusion(f32[16,192,48]{1,2,0:T(8,128)S(1)} %copy.18, f32[48,96]{1,0:T(8,128)S(1)} %compare_select_fusion, s32[96]{0:T(128)S(1)} %iota_add_fusion), kind=kOutput, calls=%fused_computation.4 | convolution fusion | flops 170108928 | bytes 903552 | tf_op jit(solution)/shard_map/bir,im->brm/dot_general | solution.py:72
  40.4 1.2 %convolution_multiply_fusion = f32[16,48,96]{2,1,0:T(8,128)S(1)} fusion(f32[16,192,48]{1,2,0:T(8,128)S(1)} %copy.18, f32[48,96]{1,0:T(8,128)S(1)} %compare_select_fusion, s32[96]{0:T(128)S(1)} %iota_add_fusion), kind=kOutput, calls=%fused_computation.3 | convolution fusion | flops 170108928 | bytes 903552 | tf_op jit(solution)/shard_map/bir,im->brm/dot_general | solution.py:73
  41.6 1.2 %fusion.28 = f32[192,16,48]{0,2,1:T(8,128)S(1)} fusion(f32[16,48,96]{2,1,0:T(8,128)S(1)} %convolution_multiply_fusion.1, s32[96]{0:T(128)S(1)} %iota_add_fusion), kind=kOutput, calls=%fused_computation.58 | convolution fusion | flops 170035200 | bytes 885120 | tf_op jit(solution)/shard_map/brm,im->bir/dot_general | solution.py:77
  42.8 1.2 %fusion.1 = f32[16,192,48]{1,2,0:T(8,128)S(1)} fusion(f32[192,16,48]{0,2,1:T(8,128)S(1)} %fusion.28, f32[16,48,96]{2,1,0:T(8,128)S(1)} %convolution_multiply_fusion, f32[48]{0:T(128)S(1)} %dynamic_slice.7, s32[96]{0:T(128)S(1)} %iota_add_fusion), kind=kOutput, calls=%fused_computation.2 | convolution fusion | flops 170330112 | bytes 1475136 | tf_op jit(solution)/shard_map/brm,im->bir/dot_general | solution.py:79
  44.0 0.8 %copy.20 = f32[16,192,48]{2,0,1:T(8,128)S(1)} copy(f32[16,192,48]{1,2,0:T(8,128)S(1)} %fusion.1) | data formatting | bytes 1179648 | tf_op jit(solution)/shard_map/mul | solution.py:111
  44.8 2.4 %reshape.74 = f32[16,1,9216]{2,1,0:T(1,128)} reshape(f32[192,16,48]{2,1,0:T(8,128)S(1)} %bitcast.109) | data formatting | bytes 1179648
  47.2 4.4 %all-to-all-start.1 = ((f32[16,1,9216]{2,1,0:T(1,128)}), f32[16,1,9216]{2,1,0:T(1,128)S(1)}, u32[]{:S(2)}, u32[]{:S(2)}) async-start(f32[16,1,9216]{2,1,0:T(1,128)} %reshape.74), calls=%async_computation.1 | async-start | bytes 1179648 | tf_op jit(solution)/shard_map/all_to_all | solution.py:113
  51.8 15.4 %all-to-all-done.1 = f32[16,1,9216]{2,1,0:T(1,128)S(1)} async-done(((f32[16,1,9216]{2,1,0:T(1,128)}), f32[16,1,9216]{2,1,0:T(1,128)S(1)}, u32[]{:S(2)}, u32[]{:S(2)}) %all-to-all-start.1) | async-done | bytes 589856 | tf_op jit(solution)/shard_map/all_to_all | solution.py:113
  67.2 2.0 %reduce.1 = f32[16,9216]{1,0:T(8,128)S(1)} reduce(f32[16,1,9216]{2,1,0:T(1,128)S(1)} %all-to-all-done.1, f32[]{:T(128)} %broadcast.105), dimensions={1}, to_apply=%all_to_all.17.reduce_sub_computation | reduce | bytes 1179652 | tf_op jit(solution)/shard_map/all_to_all | solution.py:113
  69.2 0.7 reshape.75
  69.9 0.9 %copy.21 = f32[16,12,16,48]{3,2,0,1:T(8,128)S(1)} copy(f32[16,12,16,48]{3,0,1,2:T(8,128)S(1)} %bitcast.110) | data formatting | bytes 1179648 | tf_op jit(solution)/shard_map/all_to_all | solution.py:113
  70.8 1.3 %all_to_all.20 = f32[8,2,12,768]{3,1,0,2:T(2,128)S(1)} reshape(f32[16,12,16,48]{3,2,0,1:T(8,128)S(1)} %copy.21) | data formatting | bytes 1179648 | tf_op jit(solution)/shard_map/all_to_all | solution.py:113
  72.5 0.7 multiply_subtract_fusion
  73.1 0.5 pad_maximum_fusion.4
  73.7 0.9 %copy.22 = f32[8,2,12,768]{3,1,2,0:T(2,128)} copy(f32[8,2,12,768]{3,1,0,2:T(2,128)S(1)} %pad_maximum_fusion.4) | data formatting | bytes 1179648 | tf_op jit(solution)/shard_map/stack | solution.py:56
  (44 shorter events, 2.1 us)
Async XLA Ops:
  0.0 8.3 %copy-start.5 = (f32[2,12,768]{2,0,1:T(2,128)S(1)}, f32[2,12,768]{2,0,1:T(2,128)}, u32[]{:S(2)}) copy-start(f32[2,12,768]{2,0,1:T(2,128)} %param.8) | copy-start | bytes 221188
  0.0 8.4 %copy-start = (f32[8,2,12,768]{3,1,2,0:T(2,128)S(1)}, f32[8,2,12,768]{3,1,2,0:T(2,128)}, u32[]{:S(2)}) copy-start(f32[8,2,12,768]{3,1,2,0:T(2,128)} %param.6) | copy-start | bytes 1769476
  1.0 7.9 %collective-permute-start = (f32[9,2,1,768]{3,1,0,2:T(2,128)S(1)}, f32[9,2,1,768]{3,1,0,2:T(2,128)S(1)}, u32[]{:S(2)}, u32[]{:S(2)}) collective-permute-start(f32[9,2,1,768]{3,1,0,2:T(2,128)S(1)} %get-tuple-element.9), channel_id=1, source_target_pairs={{0,1},{1,2},{2,3},{3,4},{4,5},{5,6},{6,7},{7,8},{8,9},{9,10},{10,1... | collective-permute-start | bytes 165896 | tf_op jit(solution)/shard_map/ppermute | solution.py:21
  1.5 7.4 %collective-permute-start.1 = (f32[9,2,1,768]{3,1,0,2:T(2,128)S(1)}, f32[9,2,1,768]{3,1,0,2:T(2,128)S(1)}, u32[]{:S(2)}, u32[]{:S(2)}) collective-permute-start(f32[9,2,1,768]{3,1,0,2:T(2,128)S(1)} %get-tuple-element.10), channel_id=1, source_target_pairs={{1,0},{2,1},{3,2},{4,3},{5,4},{6,5},{7,6},{8,7},{9,8},{10,9},{11,1... | collective-permute-start | bytes 165896 | tf_op jit(solution)/shard_map/ppermute | solution.py:22
  8.4 0.9 %copy-start.3 = (f32[2,12,768]{2,0,1:T(2,128)S(1)}, f32[2,12,768]{2,0,1:T(2,128)}, u32[]{:S(2)}) copy-start(f32[2,12,768]{2,0,1:T(2,128)} %param.7) | copy-start | bytes 221188
  10.5 1.2 %copy-start.1 = (f32[8,2,12,768]{3,1,0,2:T(2,128)}, f32[8,2,12,768]{3,1,0,2:T(2,128)S(1)}, u32[]{:S(2)}) copy-start(f32[8,2,12,768]{3,1,0,2:T(2,128)S(1)} %fusion.6) | copy-start | bytes 1769476
  12.3 7.4 %copy-start.6 = (s32[768]{0:T(1024)S(1)}, s32[768]{0:T(1024)}, u32[]{:S(2)}) copy-start(s32[768]{0:T(1024)} %param.10) | copy-start | bytes 9220
  14.7 20.5 %all-to-all-start = ((f32[16,1,9216]{2,1,0:T(1,128)}), f32[16,1,9216]{2,1,0:T(1,128)S(1)}, u32[]{:S(2)}, u32[]{:S(2)}) async-start(f32[16,1,9216]{2,1,0:T(1,128)} %reshape.72), calls=%async_computation | async-start | bytes 1179648 | tf_op jit(solution)/shard_map/all_to_all | solution.py:10
  44.8 6.8 %copy-start.4 = (f32[1,12,768]{2,0,1:T(1,128)S(1)}, f32[1,12,768]{2,0,1:T(1,128)}, u32[]{:S(2)}) copy-start(f32[1,12,768]{2,0,1:T(1,128)} %param.9) | copy-start | bytes 110596
  47.2 20.0 %all-to-all-start.1 = ((f32[16,1,9216]{2,1,0:T(1,128)}), f32[16,1,9216]{2,1,0:T(1,128)S(1)}, u32[]{:S(2)}, u32[]{:S(2)}) async-start(f32[16,1,9216]{2,1,0:T(1,128)} %reshape.74), calls=%async_computation.1 | async-start | bytes 1179648 | tf_op jit(solution)/shard_map/all_to_all | solution.py:113
  70.8 1.3 %copy-start.2 = (f32[8,2,12,768]{3,1,0,2:T(2,128)S(1)}, f32[8,2,12,768]{3,1,0,2:T(2,128)}, u32[]{:S(2)}) copy-start(f32[8,2,12,768]{3,1,0,2:T(2,128)} %copy-done.1) | copy-start | bytes 1769476
